TPU v7x, 256 devices: a whole 4x4x8 slice. The times are simulated.
256 devices in a mesh: img: 4 (over y_hi, core), row: 8 (over z), col: 8 (over y_lo, x).
Axes of the slice: x: 4, y: 4 (y_hi: 2, y_lo: 2; y = y_hi * 2 + y_lo), z: 8, core: 2. Of those that a mesh axis runs over, the one named last changes fastest.
Arguments:
- fresh: bfloat16 [256, 128, 640], P(('img', 'row'), 'col'), parts along dimension 0, may hold values from -16 to 16
- stale_conv_in: bfloat16 [256, 128, 640], P(('img', 'row'), 'col'), parts along dimension 0, may hold values from -6 to 6
- stale_normed: bfloat16 [256, 128, 640], P(('img', 'row'), 'col'), parts along dimension 0, may hold values from -6 to 6
- norm_gain: float32 [640], replicated, may hold values from 0.5 to 1.5
- conv_weight: bfloat16 [3, 3, 640, 640], replicated, may hold values from -0.078125 to 0.078125
- attn_gain: float32 [640], replicated, may hold values from 0.5 to 1.5
- w_query: bfloat16 [640, 640], replicated, may hold values from -3 to 3
- w_key: bfloat16 [640, 640], replicated, may hold values from -3 to 3
- w_value: bfloat16 [640, 640], replicated, may hold values from -0.25 to 0.25
- w_out: bfloat16 [640, 640], replicated, may hold values from -0.625 to 0.625
Outputs:
- result: bfloat16 [256, 128, 640], P(('img', 'row'), 'col'), parts along dimension 0
There are 4 independent parts, one for each index of `img`. A program takes and returns all parts, laid end to end along the dimension named above; an argument that names none is the same for every part. Nothing has to cross between parts.
All inputs are finite; a program needn't handle non-finite values.
Results may differ from a plain program's by a relative error of at most 0.017.
The roundings to bfloat16 on the way count: a program that leaves them out, or rounds other values in their place, can miss the bound.
Values may be sent and summed in bfloat16 or wider, within the bound.
A program may use at most 128 MiB of HBM per device.

v0:
```python
import jax
import jax.numpy as jnp
from jax import lax
from jax.sharding import PartitionSpec as P

GROUPS = 32
HEAD = 64


def with_halo(value, sides, width):
    for axis, dim in sides:
        devices, length = (lax.axis_size(axis), value.shape[dim])
        up = [(i, (i + 1) % devices) for i in range(devices - 1)]
        down = [(j, i) for i, j in up]
        last = lax.slice_in_dim(value, length - width, length, axis=dim)
        first = lax.slice_in_dim(value, 0, width, axis=dim)
        before = lax.ppermute(last, axis, up)
        after = lax.ppermute(first, axis, down)
        value = jnp.concatenate([before, value, after], axis=dim)
    return value


def attend_block(state, heads_query, keys, values, keep):
    largest, denom, summed = state
    count = keys.shape[0]
    heads_key = keys.reshape(count, heads_query.shape[1], heads_query.shape[2])
    heads_value = values.reshape(count, heads_query.shape[1], heads_query.shape[2])
    score = (
        jnp.einsum("qhd,khd->hqk", heads_query, heads_key, preferred_element_type=jnp.float32)
        * 0.125
    )
    score = jnp.where(keep[None, None, :], score, -1e30)
    new_top = jnp.maximum(largest, jnp.max(score, axis=-1))
    factor = jnp.exp(largest - new_top)
    expo = jnp.exp(score - new_top[:, :, None])
    denom = denom * factor + jnp.sum(expo, axis=-1)
    summed = summed * factor[:, :, None] + jnp.einsum(
        "hqk,khd->hqd", expo.astype(jnp.bfloat16), heads_value, preferred_element_type=jnp.float32
    )
    return (new_top, denom, summed)


def fold_rows(state, heads_query, rows, me, tok, make_kv):
    count = rows[0].shape[0]
    positions = jnp.arange(count, dtype=jnp.int32)
    keep = positions // tok != me
    step_rows = 2048
    blocks = tuple((r.reshape(count // step_rows, step_rows, r.shape[1]) for r in rows))
    keeps = keep.reshape(count // step_rows, step_rows)

    def one_block(carry, items):
        pieces, mask_row = items
        keys, values = make_kv(pieces)
        return (attend_block(carry, heads_query, keys, values, mask_row), None)

    state, unused = lax.scan(one_block, state, (blocks, keeps))
    return state


def on_device(
    fresh,
    stale_conv_in,
    stale_normed,
    norm_gain,
    conv_weight,
    attn_gain,
    w_query,
    w_key,
    w_value,
    w_out,
):
    rows_p, cols_p, width = fresh.shape
    tok = rows_p * cols_p
    per_group = width // GROUPS
    x = fresh.astype(jnp.float32)
    grouped = x.reshape(rows_p, cols_p, GROUPS, per_group)
    sums, squares = lax.psum(
        (jnp.sum(grouped, axis=(0, 1, 3)), jnp.sum(grouped * grouped, axis=(0, 1, 3))),
        ("row", "col"),
    )
    count = tok * lax.axis_size("row") * lax.axis_size("col") * per_group
    mean_g = sums / count
    var_g = squares / count - mean_g * mean_g
    normed_g = (grouped - mean_g[None, None, :, None]) * lax.rsqrt(var_g + 1e-05)[
        None, None, :, None
    ]
    conv_in = jax.nn.silu(normed_g.reshape(rows_p, cols_p, width) * norm_gain).astype(jnp.bfloat16)
    extended = with_halo(stale_conv_in, (("row", 0), ("col", 1)), 1)
    extended = extended.at[1:-1, 1:-1].set(conv_in)
    total = jnp.zeros((tok, width), jnp.float32)
    for tap_a in range(3):
        for tap_b in range(3):
            window = extended[tap_a : tap_a + rows_p, tap_b : tap_b + cols_p].reshape(tok, width)
            total = total + jnp.dot(
                window, conv_weight[tap_a, tap_b], preferred_element_type=jnp.float32
            )
    hidden = x.reshape(tok, width) + total
    mean = jnp.mean(hidden, axis=-1, keepdims=True)
    var = jnp.mean((hidden - mean) ** 2, axis=-1, keepdims=True)
    normed = ((hidden - mean) * lax.rsqrt(var + 1e-05) * attn_gain).astype(jnp.bfloat16)
    head_count = width // HEAD
    query = jnp.dot(normed, w_query, preferred_element_type=jnp.float32).astype(jnp.bfloat16)
    own_key = jnp.dot(normed, w_key, preferred_element_type=jnp.float32).astype(jnp.bfloat16)
    own_value = jnp.dot(normed, w_value, preferred_element_type=jnp.float32).astype(jnp.bfloat16)
    heads_query = query.reshape(tok, head_count, HEAD)
    start_state = (
        jnp.full((head_count, tok), -1e30, jnp.float32),
        jnp.zeros((head_count, tok), jnp.float32),
        jnp.zeros((head_count, tok, HEAD), jnp.float32),
    )
    state = attend_block(start_state, heads_query, own_key, own_value, jnp.ones((tok,), bool))
    me = lax.axis_index(("row", "col"))
    previous = stale_normed.reshape(tok, width)
    stale_key = jnp.dot(previous, w_key, preferred_element_type=jnp.float32).astype(jnp.bfloat16)
    stale_value = jnp.dot(previous, w_value, preferred_element_type=jnp.float32).astype(
        jnp.bfloat16
    )

    def given_kv(pieces):
        return (pieces[0], pieces[1])

    state = fold_rows(
        state,
        heads_query,
        (
            lax.all_gather(stale_key, ("row", "col"), axis=0, tiled=True),
            lax.all_gather(stale_value, ("row", "col"), axis=0, tiled=True),
        ),
        me,
        tok,
        given_kv,
    )
    largest, denom, summed = state
    attended = (
        (summed / denom[:, :, None]).transpose(1, 0, 2).reshape(tok, width).astype(jnp.bfloat16)
    )
    projected = jnp.dot(attended, w_out, preferred_element_type=jnp.float32)
    return (hidden + projected).astype(jnp.bfloat16).reshape(rows_p, cols_p, width)


def solution(mesh):
    placed = (
        P(("img", "row"), "col", None),
        P(("img", "row"), "col", None),
        P(("img", "row"), "col", None),
        P(),
        P(),
        P(),
        P(),
        P(),
        P(),
        P(),
    )
    return jax.shard_map(
        on_device,
        mesh=mesh,
        in_specs=placed,
        out_specs=P(("img", "row"), "col", None),
        check_vma=False,
    )
```

profile of v0, /device:TPU:16, one launch (start us, length us, event | category | flops | bytes accessed | tf_op | source)
XLA Modules:
  0.0 753.0 jit_solution(7040961664918049854)
XLA Ops:
  6.5 2.3 convolution_convert_fusion
  8.9 1.9 convolution_convert_fusion.1
  10.8 0.8 fusion.43
  11.6 1.3 collective-permute-start.1
  12.8 4.5 collective-permute-start
  17.4 1.0 convert_reduce_fusion
  18.8 159.6 %all-reduce = (f32[32]{0:T(128)S(1)}, f32[32]{0:T(128)S(1)}) all-reduce(f32[32]{0:T(128)S(1)} %reduce_sum.73, f32[32]{0:T(128)S(1)} %reduce_sum.70), channel_id=1, replica_groups=mesh['img'=4,'row'=8,'col'=8] {'row','col'}, use_global_device_ids=true, to_apply=%region_5.6 | all-reduce | flops 64 | bytes 512 | tf_op jit(solution)/shard_map/psum | solution.py:77
  178.7 1.0 multiply_convert_fusion.1
  179.8 0.9 constant_dynamic-update-slice_fusion.1
  180.8 1.3 collective-permute-start.2
  182.1 1.3 collective-permute-start.3
  183.6 4.2 collective-permute-done.3
  188.0 2.6 scatter.4
  190.8 1.6 fusion.21
  192.4 2.1 convolution_add_fusion.9
  194.5 1.5 convolution_add_fusion.8
  196.1 1.5 convolution_add_fusion.7
  201.5 1.0 convolution_add_fusion
  202.5 128.7 %all-gather.5.cloned.1.call-done = bf16[8192,640]{1,0:T(8,128)(2,1)} async-done(((bf16[128,640]{1,0:T(8,128)(2,1)}), bf16[8192,640]{1,0:T(8,128)(2,1)}) %all-gather.5.cloned.1.call-update) | async-done | bytes 10485776 | tf_op jit(solution)/shard_map/all_gather | solution.py:127
  331.2 318.4 %all-gather.3.cloned.1.call-done = bf16[8192,640]{1,0:T(8,128)(2,1)} async-done(((bf16[128,640]{1,0:T(8,128)(2,1)}), bf16[8192,640]{1,0:T(8,128)(2,1)}) %all-gather.3.cloned.1.call-update) | async-done | bytes 10485776 | tf_op jit(solution)/shard_map/all_gather | solution.py:126
  649.6 93.4 %while.15 = (s32[]{:T(128)}, f32[10,128]{1,0:T(8,128)S(1)}, f32[10,128]{1,0:T(8,128)S(1)}, f32[10,128,64]{1,2,0:T(8,128)}, pred[4,2048]{1,0:T(4,128)(4,1)S(1)}, ...) while((s32[]{:T(128)}, f32[10,128]{1,0:T(8,128)S(1)}, ...), condition=%wide.region_13.14_spmd, body=%wide.region_10.13_spmd.sunk | while | flops 700090880 | bytes 73001208 | solution.py:56
  649.6 5.3 constant_dynamic-slice_fusion.3
  655.0 3.0 copy.32
  658.0 4.6 copy.33
  662.5 3.7 bitcast_reduce_fusion.2
  666.2 2.9 fusion.80
  669.2 3.0 fusion.81
  672.2 0.7 copy-done.9
  673.0 5.3 constant_dynamic-slice_fusion.3
  678.3 3.0 copy.32
  681.3 4.6 copy.33
  685.9 3.7 bitcast_reduce_fusion.2
  689.6 2.9 fusion.80
  692.6 3.0 fusion.81
  696.3 5.3 constant_dynamic-slice_fusion.3
  701.7 3.0 copy.32
  704.6 4.6 copy.33
  709.2 3.7 bitcast_reduce_fusion.2
  712.9 2.9 fusion.80
  715.9 3.0 fusion.81
  719.7 5.3 constant_dynamic-slice_fusion.3
  725.0 3.0 copy.32
  728.0 4.6 copy.33
  732.6 3.7 bitcast_reduce_fusion.2
  736.3 2.9 fusion.80
  739.2 3.0 fusion.81
  743.0 1.0 divide_convert_fusion
  744.0 2.2 fusion.12
  (109 shorter events, 7.7 us)
Async XLA Ops:
  6.5 2.3 copy-start
  6.5 324.7 %all-gather.5.cloned.1.call-start = ((), (), s32[]{:S(2)}) async-start(), calls=%async_computation.1 | async-start | bytes 10649600 | tf_op jit(solution)/shard_map/all_gather | solution.py:127
  8.8 640.8 %all-gather.3.cloned.1.call-start = ((), (), s32[]{:S(2)}) async-start(), calls=%async_computation | async-start | bytes 10649600 | tf_op jit(solution)/shard_map/all_gather | solution.py:126
  11.6 169.2 %collective-permute-start.1 = (bf16[1,16,640]{2,1,0:T(8,128)(2,1)S(1)}, bf16[1,16,640]{2,1,0:T(8,128)(2,1)S(1)}, u32[]{:S(2)}, u32[]{:S(2)}) collective-permute-start(bf16[1,16,640]{2,1,0:T(8,128)(2,1)S(1)} %get-tuple-element.114), channel_id=1, source_target_pairs={{8,0},{16,8},{24,16},{32,24},{40,32},{48,40},{56,48},{9,1},{17,9},... | collective-permute-start | bytes 61448 | tf_op jit(solution)/shard_map/ppermute | solution.py:18
  12.8 166.9 %collective-permute-start = (bf16[1,16,640]{2,1,0:T(8,128)(2,1)S(1)}, bf16[1,16,640]{2,1,0:T(8,128)(2,1)S(1)}, u32[]{:S(2)}, u32[]{:S(2)}) collective-permute-start(bf16[1,16,640]{2,1,0:T(8,128)(2,1)S(1)} %get-tuple-element.115), channel_id=1, source_target_pairs={{0,8},{8,16},{16,24},{24,32},{32,40},{40,48},{48,56},{1,9},{9,17},... | collective-permute-start | bytes 61448 | tf_op jit(solution)/shard_map/ppermute | solution.py:17
  180.8 2.8 collective-permute-start.2
  182.1 5.7 collective-permute-start.3
  190.6 6.9 copy-start.5
  190.6 8.2 %copy-start.7 = (bf16[8,16,640]{2,1,0:T(8,128)(2,1)S(1)}, bf16[8,16,640]{2,1,0:T(8,128)(2,1)}, u32[]{:S(2)}) copy-start(bf16[8,16,640]{2,1,0:T(8,128)(2,1)} %param.14) | copy-start | bytes 491524
  190.8 8.7 %copy-start.11 = (f32[640]{0:T(1024)S(1)}, f32[640]{0:T(1024)}, u32[]{:S(2)}) copy-start(f32[640]{0:T(1024)} %param.19) | copy-start | bytes 7684
  192.4 7.6 %copy-start.6 = (bf16[640,640]{1,0:T(8,128)(2,1)S(1)}, bf16[640,640]{1,0:T(8,128)(2,1)}, u32[]{:S(2)}) copy-start(bf16[640,640]{1,0:T(8,128)(2,1)} %param.22) | copy-start | bytes 2457604
  194.5 6.0 copy-start.10
  199.2 450.4 %copy-start.2 = (f32[128,640]{1,0:T(8,128)}, f32[128,640]{1,0:T(8,128)S(1)}, u32[]{:S(2)}) copy-start(f32[128,640]{1,0:T(8,128)S(1)} %get-tuple-element.121) | copy-start | bytes 983044
  649.6 5.4 copy-start.3
  666.2 3.0 copy-start.1
  666.2 3.0 copy-start.8
  669.2 3.7 copy-start.4
  672.2 0.7 copy-start.9
  672.9 5.4 copy-start.3
  689.5 3.0 copy-start.1
  689.6 3.0 copy-start.8
  692.5 3.7 copy-start.4
  695.5 0.7 copy-start.9
  696.3 5.4 copy-start.3
  712.9 3.0 copy-start.1
  712.9 3.0 copy-start.8
  715.9 3.7 copy-start.4
  718.9 0.7 copy-start.9
  719.6 5.4 copy-start.3
  736.2 3.0 copy-start.1
  736.2 3.0 copy-start.8
  739.2 3.7 copy-start.4
  742.2 0.7 copy-start.9
Sparse Core Ops, SparseCore 0:
  9.1 322.0 all-gather.4
  333.0 316.5 all-gather.2
where the time goes:
time: 754 us; the launch traced here: 753 us
  waiting for transfers between devices  451 us (60%)
  blocking collectives  160 us (21%)
  local copies, waits for them, and re-layouts  60.2 us (8%)
  matrix products  43.7 us (6%)
  other arithmetic  15.5 us (2%)
  between operations  13.8 us (2%)
  starting transfers between devices  8.45 us (1%)
    all_gather x1, waiting for transfers between devices, on_device(): lax.all_gather(stale_key, ('row', 'col'), axis=0, tiled=True)  318 us
    psum x1, blocking collectives, on_device(): lax.psum((jnp.sum(grouped, axis=(0, 1, 3)), jnp.sum(grouped * grouped, ax...  160 us
    all_gather x1, waiting for transfers between devices, on_device(): lax.all_gather(stale_value, ('row', 'col'), axis=0, tiled=True)  129 us
    dynamic_slice x16, local copies, waits for them, and re-layouts, fold_rows(): state, unused = lax.scan(one_block, state, (blocks, keeps))  51.8 us
  transfers between devices with their start and end apart: 6, of which 4 were waited for; matrix products, arithmetic and copies ran while one was open for 3% of the time, Pallas kernels for 0%

commit v1 on v0

v1 whole, which is shorter than its diff:
```python
import functools
import jax
import jax.numpy as jnp
from jax import lax
from jax.experimental import pallas as pl
from jax.experimental.pallas import tpu as pltpu
from jax.sharding import PartitionSpec as P

GROUPS = 32
HEAD = 64
C = 640
TOK = 128
PW = 16
NZ = 8
NX = 4
NCOL = 8
PAIRS = 5
KROWS = 17 * TOK
SPAN = 16 * TOK
LOG2E = 1.4426950408889634
MESH = pl.DeviceIdType.MESH
F32 = jnp.float32
BF16 = jnp.bfloat16
HIGH = lax.Precision.HIGHEST
NT = (((1,), (1,)), ((), ()))
TN = (((0,), (0,)), ((), ()))


def iota(shape, dim):
    return lax.broadcasted_iota(jnp.int32, shape, dim)


def kernel(
    fresh_h, sci_h, sn_h, ngain, again, wc_h, wq_h, wk_h, wv_h, wo_h,
    out_ref,
    fresh, sci, wc, wq, wkv, wo,
    st_send, st_recv,
    colbuf, ext, xw,
    sb, kall, vx, hid,
    q_mine, q_recv, part, ret_a, lse, ret_l,
    load_sem, st_ssem, st_rsem, halo_ssem, halo_rsem,
    zo_ssem, zo_rsem, zp_ssem, zp_rsem, y_ssem, y_rsem,
    q_ssem, q_rsem, a_ssem, a_rsem, l_ssem, l_rsem,
):
    r = lax.axis_index("row")
    c = lax.axis_index("col")
    x = lax.rem(c, NX)
    ybase = c - x
    rown = [lax.rem(r + j, NZ) for j in range(NZ)]
    coln = [lax.rem(c + j, NCOL) for j in range(NCOL)]
    xn = [ybase + lax.rem(x + j, NX) for j in range(NX)]
    ypart = lax.rem(c + NX, NCOL)

    def remote(src, dst, ss, rs, dev):
        return pltpu.make_async_remote_copy(
            src_ref=src, dst_ref=dst, send_sem=ss, recv_sem=rs,
            device_id=dev, device_id_type=MESH)

    loads = [
        pltpu.make_async_copy(fresh_h, fresh, load_sem.at[0]),
        pltpu.make_async_copy(sn_h, sb.at[0, pl.ds(0, TOK)], load_sem.at[1]),
        pltpu.make_async_copy(sci_h, sci, load_sem.at[2]),
        pltpu.make_async_copy(wk_h, wkv.at[:, pl.ds(0, C)], load_sem.at[3]),
        pltpu.make_async_copy(wv_h, wkv.at[:, pl.ds(C, C)], load_sem.at[4]),
        pltpu.make_async_copy(wc_h, wc, load_sem.at[5]),
        pltpu.make_async_copy(wq_h, wq, load_sem.at[6]),
        pltpu.make_async_copy(wo_h, wo, load_sem.at[7]),
    ]
    for cp in loads:
        cp.start()

    barrier = pltpu.get_barrier_semaphore()
    partners = [{"row": rown[j]} for j in range(1, NZ)]
    partners += [{"col": coln[j]} for j in range(1, NCOL)]
    partners += [{"row": rown[i], "col": coln[j]} for i in (1, NZ - 1) for j in (1, NCOL - 1)]
    for dev in partners:
        pl.semaphore_signal(barrier, inc=1, device_id=dev, device_id_type=MESH)

    loads[0].wait()
    xf = fresh[...].astype(F32)
    s1 = jnp.sum(xf, axis=0, keepdims=True)
    s2 = jnp.sum(xf * xf, axis=0, keepdims=True)
    row8 = iota((8, C), 0)
    st = jnp.where(row8 == 0, s1, jnp.where(row8 == 1, s2, 0.0))
    per = C // GROUPS
    gc = iota((C, 128), 0)
    gl = iota((C, 128), 1) * per
    gmat = jnp.where((gc >= gl) & (gc < gl + per), 1.0, 0.0).astype(F32)
    st_send[0] = jnp.dot(st, gmat, precision=HIGH, preferred_element_type=F32)
    loads[2].wait()
    e0 = iota((16, TOK), 0)
    e1 = iota((16, TOK), 1)
    want = jnp.where(e0 < 8, e0 * PW, (e0 - 8) * PW + PW - 1)
    sel = jnp.where(e1 == want, 1.0, 0.0).astype(BF16)
    colbuf[...] = jnp.dot(sel, sci[...], preferred_element_type=F32).astype(BF16)
    loads[1].wait()

    pl.semaphore_wait(barrier, len(partners))

    def stat_copies(stage):
        devs = [{"row": rown[j]} if stage == 0 else {"col": coln[j]} for j in range(1, 8)]
        return [remote(st_send.at[stage], st_recv.at[stage, j], st_ssem.at[stage, j], st_rsem.at[stage, j], dev)
                for j, dev in enumerate(devs)]

    stat1 = stat_copies(0)
    for cp in stat1:
        cp.start()

    up, down = {"row": rown[1]}, {"row": rown[NZ - 1]}

    def own_copy(step, plus):
        src = step - 1 if plus else (0 if step == 1 else 3 + step)
        dst = step if plus else 4 + step
        i = step - 1 + (0 if plus else 4)
        return remote(sb.at[src, pl.ds(0, TOK)], sb.at[dst, pl.ds(0, TOK)],
                      zo_ssem.at[i], zo_rsem.at[i], up if plus else down)

    def half_copy(step, plus):
        src = step - 1 if plus else (0 if step == 1 else 3 + step)
        dst = step if plus or step == 4 else 4 + step
        i = step - 1 + (0 if plus else 4)
        return remote(sb.at[src, pl.ds(TOK, 64)], sb.at[dst, pl.ds(TOK, 64)],
                      zp_ssem.at[i], zp_rsem.at[i], up if plus else down)

    def y_copy(slot):
        return remote(sb.at[slot, pl.ds(64, 64)], sb.at[slot, pl.ds(TOK + 64, 64)],
                      y_ssem.at[slot], y_rsem.at[slot], {"col": ypart})

    y_first = remote(sb.at[0, pl.ds(0, 64)], sb.at[0, pl.ds(TOK, 64)],
                     y_ssem.at[8], y_rsem.at[8], {"col": ypart})
    own_p = {s: own_copy(s, True) for s in range(1, 5)}
    own_m = {s: own_copy(s, False) for s in range(1, 4)}
    half_p = {s: half_copy(s, True) for s in range(1, 4)}
    half_m = {s: half_copy(s, False) for s in range(1, 5)}
    ys = {s: y_copy(s) for s in range(8)}
    y_first.start()
    own_p[1].start()
    own_m[1].start()

    lft, rgt = coln[NCOL - 1], coln[1]
    upr, dnr = rown[NZ - 1], rown[1]
    top, bot = sci.at[pl.ds(0, 16)], sci.at[pl.ds(TOK - 16, 16)]
    plan = [
        (top, 144, {"row": upr}), (top, 240, {"row": upr, "col": lft}), (top, 224, {"row": upr, "col": rgt}),
        (bot, 0, {"row": dnr}), (bot, 208, {"row": dnr, "col": lft}), (bot, 192, {"row": dnr, "col": rgt}),
        (colbuf, 176, {"col": lft}), (colbuf, 160, {"col": rgt}),
    ]
    halos = [remote(src, ext.at[pl.ds(at, 16)], halo_ssem.at[i], halo_rsem.at[i], dev)
             for i, (src, at, dev) in enumerate(plan)]
    for cp in halos:
        cp.start()
    ys[0].start()

    for p in range(PAIRS):
        vx[:, 256 * p + 128:256 * p + 256] = jnp.ones((KROWS, 128), BF16)

    def project(block, rows):
        kv = jnp.dot(block, wkv[...], preferred_element_type=F32).astype(BF16)
        for i, row in enumerate(rows):
            piece = kv[i * TOK:(i + 1) * TOK]
            kall[row:row + TOK, :] = piece[:, :C]
            for p in range(PAIRS):
                vx[row:row + TOK, 256 * p:256 * p + 128] = piece[:, C + 128 * p:C + 128 * p + 128]

    def own_rows(slot):
        return sb[slot, 0:TOK]

    def far_rows(slot):
        return sb[slot, TOK:2 * TOK]

    loads[3].wait()
    loads[4].wait()
    project(own_rows(0), [16 * TOK])

    tot = st_send[0]
    for j, cp in enumerate(stat1):
        cp.wait_recv()
        tot = tot + st_recv[0, j]
    st_send[1] = tot
    stat2 = stat_copies(1)
    for cp in stat2:
        cp.start()
    y_first.wait_recv()
    half_p[1].start()
    half_m[1].start()

    pe = iota((160, 256), 0)
    ps = iota((160, 256), 1)
    pi = lax.shift_right_logical(pe, 4)
    pj = pe & 15
    inner = (pi > 0) & (pi < 9)
    vert = ((pi > 0) | (r > 0)) & ((pi < 9) | (r < NZ - 1))
    left_src = jnp.where(pj > 0, pe - 1, jnp.where(inner, 167 + pi, jnp.where(pi == 0, 207, 239)))
    right_src = jnp.where(pj < 15, pe + 1, jnp.where(inner, 175 + pi, jnp.where(pi == 0, 208, 240)))
    left_ok = vert & ((pj > 0) | (c > 0))
    right_ok = vert & ((pj < 15) | (c < NCOL - 1))
    sel_left = jnp.where(left_ok & (ps == left_src), 1.0, 0.0).astype(BF16)
    sel_right = jnp.where(right_ok & (ps == right_src), 1.0, 0.0).astype(BF16)

    own_p[1].wait_recv()
    own_m[1].wait_recv()
    own_p[2].start()
    own_m[2].start()
    ys[1].start()
    ys[5].start()
    project(jnp.concatenate([own_rows(1), own_rows(5)], axis=0), [TOK, 5 * TOK])

    tot = st_send[1]
    for j, cp in enumerate(stat2):
        cp.wait_recv()
        tot = tot + st_recv[1, j]
    count = TOK * NZ * NCOL * per
    mom = tot * (1.0 / count)
    mean_g = mom[0:1]
    var_g = mom[1:2] - mean_g * mean_g
    rstd_g = lax.rsqrt(var_g + 1e-05)
    row8 = iota((8, 128), 0)
    both = jnp.where(row8 == 0, mean_g, jnp.where(row8 == 1, rstd_g, 0.0))
    hl = iota((128, C), 0) * per
    hc = iota((128, C), 1)
    gback = jnp.where((hc >= hl) & (hc < hl + per), 1.0, 0.0).astype(F32)
    wide = jnp.dot(both, gback, precision=HIGH, preferred_element_type=F32)
    xf = fresh[...].astype(F32)
    v = (xf - wide[0:1]) * wide[1:2] * ngain[...]
    ext[16:16 + TOK, :] = (v * (1.0 / (1.0 + jnp.exp(-v)))).astype(BF16)
    for cp in halos:
        cp.wait_recv()
    zero = jnp.zeros((16, C), BF16)
    ext[0:16, :] = jnp.where(r > 0, ext[0:16, :], zero)
    ext[144:160, :] = jnp.where(r < NZ - 1, ext[144:160, :], zero)
    whole = ext[...]
    e_left = jnp.dot(sel_left, whole, preferred_element_type=F32).astype(BF16)
    e_right = jnp.dot(sel_right, whole, preferred_element_type=F32).astype(BF16)
    for a in range(3):
        xw[:, (3 * a) * C:(3 * a + 1) * C] = e_left[16 * a:16 * a + TOK]
        xw[:, (3 * a + 1) * C:(3 * a + 2) * C] = ext[16 * a:16 * a + TOK, :]
        xw[:, (3 * a + 2) * C:(3 * a + 3) * C] = e_right[16 * a:16 * a + TOK]
    loads[5].wait()
    hidden = xf + jnp.dot(xw[...], wc[...], preferred_element_type=F32)
    hid[...] = hidden
    mean = jnp.mean(hidden, axis=-1, keepdims=True)
    cen = hidden - mean
    var = jnp.mean(cen * cen, axis=-1, keepdims=True)
    normed = (cen * lax.rsqrt(var + 1e-05) * again[...]).astype(BF16)
    loads[6].wait()
    q_mine[...] = (jnp.dot(normed, wq[...], preferred_element_type=F32) * (LOG2E / 8)).astype(BF16)
    q_cp = {j: remote(q_mine, q_recv.at[NX - j - 1], q_ssem.at[j - 1], q_rsem.at[NX - j - 1], {"col": xn[j]})
            for j in (1, 3, 2)}
    for cp in q_cp.values():
        cp.start()
    project(normed, [0])

    half_p[1].wait_recv()
    half_m[1].wait_recv()
    half_p[2].start()
    half_m[2].start()
    own_p[2].wait_recv()
    own_m[2].wait_recv()
    own_p[3].start()
    own_m[3].start()
    ys[2].start()
    ys[6].start()
    project(jnp.concatenate([own_rows(2), own_rows(6)], axis=0), [2 * TOK, 6 * TOK])
    half_p[2].wait_recv()
    half_m[2].wait_recv()
    half_p[3].start()
    half_m[3].start()
    own_p[3].wait_recv()
    own_m[3].wait_recv()
    own_p[4].start()
    ys[3].start()
    ys[7].start()
    project(jnp.concatenate([own_rows(3), own_rows(7)], axis=0), [3 * TOK, 7 * TOK])
    half_m[3].wait_recv()
    half_m[4].start()
    half_p[3].wait_recv()
    for s in (0, 1, 5):
        ys[s].wait_recv()
    project(jnp.concatenate([far_rows(0), far_rows(1), far_rows(5)], axis=0), [8 * TOK, 9 * TOK, 13 * TOK])
    own_p[4].wait_recv()
    ys[4].start()
    for s in (2, 6, 3, 7):
        ys[s].wait_recv()
    project(jnp.concatenate([far_rows(s) for s in (2, 6, 3, 7)], axis=0), [(8 + s) * TOK for s in (2, 6, 3, 7)])
    half_m[4].wait_recv()
    ys[4].wait_recv()
    project(jnp.concatenate([own_rows(4), far_rows(4)], axis=0), [4 * TOK, 12 * TOK])

    lane = iota((TOK, 128), 1)

    def attend(read_q, base, write, lse_ref):
        table = jnp.zeros((TOK, 128), F32)
        for p in range(PAIRS):
            qp = read_q(p)
            zq = jnp.zeros_like(qp)
            qm = jnp.concatenate([jnp.where(lane < HEAD, qp, zq), jnp.where(lane < HEAD, zq, qp)], axis=0)
            s = lax.dot_general(qm, kall[base:base + SPAN, 128 * p:128 * p + 128], NT, preferred_element_type=F32)
            m = jnp.max(s, axis=1, keepdims=True)
            w = jnp.exp2(s - m).astype(BF16)
            o = jnp.dot(w, vx[base:base + SPAN, 256 * p:256 * p + 256], preferred_element_type=F32)
            den = o[:, 128:]
            norm = o[:, :128] / den
            write(p, jnp.where(lane < HEAD, norm[:TOK], norm[TOK:]).astype(BF16))
            ls = m + jnp.log2(den)
            table = jnp.where(lane == 2 * p, ls[:TOK], jnp.where(lane == 2 * p + 1, ls[TOK:], table))
        lse_ref[...] = table.T[:16]

    def writer(ref):
        def write(p, val):
            ref[:, 128 * p:128 * p + 128] = val
        return write

    def reader(ref):
        return lambda p: ref[:, 128 * p:128 * p + 128]

    attend(reader(q_mine), 0, writer(part.at[0]), lse.at[0])
    backs = []
    for j in (1, 3, 2):
        q_cp[NX - j].wait_recv()
        attend(reader(q_recv.at[j - 1]), TOK, writer(part.at[j]), lse.at[j])
        dst = NX - j - 1
        a_cp = remote(part.at[j], ret_a.at[dst], a_ssem.at[j - 1], a_rsem.at[dst], {"col": xn[j]})
        l_cp = remote(lse.at[j], ret_l.at[dst], l_ssem.at[j - 1], l_rsem.at[dst], {"col": xn[j]})
        a_cp.start()
        l_cp.start()
        backs += [a_cp, l_cp]
    for cp in backs:
        cp.wait_recv()

    ls = [lse[0]] + [ret_l[j] for j in range(3)]
    top_l = jnp.maximum(jnp.maximum(ls[0], ls[1]), jnp.maximum(ls[2], ls[3]))
    ws = [jnp.exp2(l - top_l) for l in ls]
    inv = 1.0 / (ws[0] + ws[1] + ws[2] + ws[3])
    eh = iota((32, C), 0) & 15
    ec = iota((32, C), 1)
    spread = jnp.where((ec >= eh * HEAD) & (ec < eh * HEAD + HEAD), 1.0, 0.0).astype(BF16)
    att = jnp.zeros((TOK, C), F32)
    for i in range(4):
        share = ws[i] * inv
        hi = share.astype(BF16)
        lo = (share - hi.astype(F32)).astype(BF16)
        split = jnp.concatenate([hi, lo], axis=0)
        full = lax.dot_general(split, spread, TN, preferred_element_type=F32)
        val = part[0] if i == 0 else ret_a[i - 1]
        att = att + full * val.astype(F32)
    loads[7].wait()
    out = hid[...] + jnp.dot(att.astype(BF16), wo[...], preferred_element_type=F32)
    out_ref[...] = out.astype(BF16)

    sends = stat1 + stat2 + halos + [y_first] + list(own_p.values()) + list(own_m.values())
    sends += list(half_p.values()) + list(half_m.values()) + list(ys.values()) + list(q_cp.values()) + backs
    for cp in sends:
        cp.wait_send()


def on_device(fresh, stale_conv_in, stale_normed, norm_gain, conv_weight, attn_gain, w_query, w_key, w_value, w_out):
    shape = fresh.shape
    flat = lambda a: a.reshape(TOK, C)
    hbm = pl.BlockSpec(memory_space=pl.ANY)
    vmem = pl.BlockSpec(memory_space=pltpu.VMEM)
    dma = pltpu.SemaphoreType.DMA
    V = pltpu.VMEM
    out = pl.pallas_call(
        kernel,
        out_shape=jax.ShapeDtypeStruct((TOK, C), BF16),
        in_specs=[hbm] * 3 + [vmem] * 2 + [hbm] * 5,
        out_specs=vmem,
        scratch_shapes=[
            V((TOK, C), BF16), V((TOK, C), BF16), V((9 * C, C), BF16), V((C, C), BF16), V((C, 2 * C), BF16), V((C, C), BF16),
            V((2, 8, 128), F32), V((2, 7, 8, 128), F32),
            V((16, C), BF16), V((256, C), BF16), V((TOK, 9 * C), BF16),
            V((NZ, 2 * TOK, C), BF16), V((KROWS, C), BF16), V((KROWS, 256 * PAIRS), BF16), V((TOK, C), F32),
            V((TOK, C), BF16), V((3, TOK, C), BF16), V((4, TOK, C), BF16), V((3, TOK, C), BF16),
            V((4, 16, 128), F32), V((3, 16, 128), F32),
            dma((8,)), dma((2, 7)), dma((2, 7)), dma((8,)), dma((8,)),
            dma((8,)), dma((8,)), dma((8,)), dma((8,)), dma((9,)), dma((9,)),
            dma((3,)), dma((3,)), dma((3,)), dma((3,)), dma((3,)), dma((3,)),
        ],
        compiler_params=pltpu.CompilerParams(
            collective_id=0, has_side_effects=True, vmem_limit_bytes=60 * 2**20),
    )(
        flat(fresh), flat(stale_conv_in), flat(stale_normed),
        norm_gain.reshape(1, C), attn_gain.reshape(1, C),
        conv_weight.reshape(9 * C, C), w_query, w_key, w_value, w_out,
    )
    return out.reshape(shape)


def solution(mesh):
    cells = P(("img", "row"), "col", None)
    return jax.shard_map(
        on_device,
        mesh=mesh,
        in_specs=(cells, cells, cells) + (P(),) * 7,
        out_specs=cells,
        check_vma=False,
    )
```

time: 754 us -> 64.4 us (0.09)
  waiting for transfers between devices: 451 us -> 0 us
  blocking collectives: 160 us -> 0 us
  Pallas kernels: 0 us -> 60.1 us
  local copies, waits for them, and re-layouts: 60.2 us -> 4.11 us
  matrix products: 43.7 us -> 0 us
  other arithmetic: 15.5 us -> 0 us
  between operations: 13.8 us -> 0.01 us
  starting transfers between devices: 8.45 us -> 0 us
    all_gather x2 -> x0, waiting for transfers between devices: 447 us -> none  [the longest x1 318 us: on_device(): lax.all_gather(stale_key, ('row', 'col'), axis=0, tiled=True)]
    psum x1 -> x0, blocking collectives: 160 us -> none  [on_device(): lax.psum((jnp.sum(grouped, axis=(0, 1, 3)), jnp.sum(grouped * grouped, ax...]
    pallas_call x0 -> x1, Pallas kernels: none -> 60.1 us  [on_device(): pl.pallas_call(kernel, out_shape=jax.ShapeDtypeStruct((TOK, C), BF16), in...]
    dynamic_slice x16 -> x0, local copies, waits for them, and re-layouts: 51.8 us -> none  [fold_rows(): state, unused = lax.scan(one_block, state, (blocks, keeps))]
    dot_general x25 -> x0, matrix products: 43.7 us -> none  [the longest x5 14.9 us: attend_block(): jnp.einsum('qhd,khd->hqk', heads_query, heads_key, preferred_element_type...]
    reduce_sum x9 -> x0, other arithmetic: 13.2 us -> none  [the longest x5 11.8 us: attend_block(): denom = denom * factor + jnp.sum(expo, axis=-1)]
    ppermute x4 -> x0, starting transfers between devices: 8.41 us -> none  [the longest x2 5.84 us: with_halo(): before = lax.ppermute(last, axis, up)]
  transfers between devices with their start and end apart: 6 -> 0, of which waited for: 4 -> 0; matrix products, arithmetic and copies ran while one was open for 3% -> 0% of each run, Pallas kernels for 0% -> 0%
where the time goes in v1:
time: 64.4 us; the launch traced here: 64.2 us
  Pallas kernels  60.1 us (93%)
  local copies, waits for them, and re-layouts  4.11 us (6%)
    pallas_call x1, Pallas kernels, on_device(): pl.pallas_call(kernel, out_shape=jax.ShapeDtypeStruct((TOK, C), BF16), in...  60.1 us
    unnamed x1, local copies, waits for them, and re-layouts  1.6 us

profile of v1, /device:TPU:16, one launch (start us, length us, event | category | flops | bytes accessed | tf_op | source)
XLA Modules:
  0.0 64.2 jit_solution(10169325741600194718)
XLA Ops:
  0.0 1.3 %reshape.24.ngain = f32[1,640]{1,0:T(1,128)} reshape(f32[640]{0:T(1024)} %param.13) | data formatting | bytes 5120 | tf_op jit(solution)/shard_map/reshape | solution.py:383
  1.3 1.2 %reshape.25.again = f32[1,640]{1,0:T(1,128)} reshape(f32[640]{0:T(1024)} %param.15) | data formatting | bytes 5120 | tf_op jit(solution)/shard_map/reshape | solution.py:383
  2.5 60.1 %shard_map.100 = bf16[128,640]{1,0:T(8,128)(2,1)} custom-call(bf16[128,640]{1,0:T(8,128)(2,1)} %bitcast.7, bf16[128,640]{1,0:T(8,128)(2,1)} %bitcast.8, bf16[128,640]{1,0:T(8,128)(2,1)} %bitcast.9, f32[1,640]{1,0:T(1,128)} %reshape.24.ngain, f32[1,640]{1,0:T(1,128)} %reshape.25.again, bf16[5760,640]{1,0:T(8,128)(2,1)} %bitcast.5, bf16[640,640]{1,0:T(8,128)(2,1)} %wq_h.1, ...), custom_call_target="tpu_custom_call" | custom-call | tf_op jit(solution)/shard_map/pallas_call | solution.py:363
  62.6 1.6 %copy.12 = bf16[8,16,640]{2,1,0:T(8,128)(2,1)} copy(bf16[8,16,640]{2,1,0:T(8,128)(2,1)} %bitcast.6) | data formatting | bytes 327680

commit v2 on v1

--- a/solution.py
+++ b/solution.py
@@ -16,7 +16,8 @@
 NCOL = 8
 PAIRS = 5
 KROWS = 17 * TOK
-SPAN = 16 * TOK
+ORDER = [None, (0, 1), (0, 5), (0, 2), (0, 6), (1, 0), (1, 1), (1, 5), (0, 0),
+         (0, 3), (0, 7), (1, 2), (1, 6), (0, 4), (1, 3), (1, 7), (1, 4)]
 LOG2E = 1.4426950408889634
 MESH = pl.DeviceIdType.MESH
 F32 = jnp.float32
@@ -37,9 +38,9 @@
     st_send, st_recv,
     colbuf, ext, xw,
     sb, kall, vx, hid,
-    q_mine, q_recv, part, ret_a, lse, ret_l,
+    q_mine, q_recv, part, ret_a, lse, ret_l, st_o, st_m,
     load_sem, st_ssem, st_rsem, halo_ssem, halo_rsem,
-    zo_ssem, zo_rsem, zp_ssem, zp_rsem, y_ssem, y_rsem,
+    z_ssem, z_rsem, y_ssem, y_rsem,
     q_ssem, q_rsem, a_ssem, a_rsem, l_ssem, l_rsem,
 ):
     r = lax.axis_index("row")
@@ -108,19 +109,12 @@
 
     up, down = {"row": rown[1]}, {"row": rown[NZ - 1]}
 
-    def own_copy(step, plus):
-        src = step - 1 if plus else (0 if step == 1 else 3 + step)
-        dst = step if plus else 4 + step
-        i = step - 1 + (0 if plus else 4)
-        return remote(sb.at[src, pl.ds(0, TOK)], sb.at[dst, pl.ds(0, TOK)],
-                      zo_ssem.at[i], zo_rsem.at[i], up if plus else down)
-
-    def half_copy(step, plus):
+    def ring_copy(stream, plus, step, first, rows):
         src = step - 1 if plus else (0 if step == 1 else 3 + step)
         dst = step if plus or step == 4 else 4 + step
-        i = step - 1 + (0 if plus else 4)
-        return remote(sb.at[src, pl.ds(TOK, 64)], sb.at[dst, pl.ds(TOK, 64)],
-                      zp_ssem.at[i], zp_rsem.at[i], up if plus else down)
+        d = 0 if plus else 1
+        return remote(sb.at[src, pl.ds(first, rows)], sb.at[dst, pl.ds(first, rows)],
+                      z_ssem.at[stream, d, step - 1], z_rsem.at[stream, d, step - 1], up if plus else down)
 
     def y_copy(slot):
         return remote(sb.at[slot, pl.ds(64, 64)], sb.at[slot, pl.ds(TOK + 64, 64)],
@@ -128,14 +122,25 @@
 
     y_first = remote(sb.at[0, pl.ds(0, 64)], sb.at[0, pl.ds(TOK, 64)],
                      y_ssem.at[8], y_rsem.at[8], {"col": ypart})
-    own_p = {s: own_copy(s, True) for s in range(1, 5)}
-    own_m = {s: own_copy(s, False) for s in range(1, 4)}
-    half_p = {s: half_copy(s, True) for s in range(1, 4)}
-    half_m = {s: half_copy(s, False) for s in range(1, 5)}
+    ring = {}
+    for stream in range(3):
+        for step in range(1, 4):
+            ring[stream, step] = [ring_copy(stream, plus, step, 64 * stream, 64) for plus in (True, False)]
+    ring[0, 4] = [ring_copy(0, True, 4, 0, 64)]
+    ring[1, 4] = [ring_copy(1, False, 4, 64, 64)]
+    ring[2, 4] = [ring_copy(2, True, 4, TOK, 32), ring_copy(2, False, 4, TOK + 32, 32)]
     ys = {s: y_copy(s) for s in range(8)}
+
+    def send(stream, step):
+        for cp in ring[stream, step]:
+            cp.start()
+
+    def arrived(stream, step):
+        for cp in ring[stream, step]:
+            cp.wait_recv()
+
+    send(0, 1)
     y_first.start()
-    own_p[1].start()
-    own_m[1].start()
 
     lft, rgt = coln[NCOL - 1], coln[1]
     upr, dnr = rown[NZ - 1], rown[1]
@@ -149,6 +154,7 @@
              for i, (src, at, dev) in enumerate(plan)]
     for cp in halos:
         cp.start()
+    send(1, 1)
     ys[0].start()
 
     for p in range(PAIRS):
@@ -162,15 +168,13 @@
             for p in range(PAIRS):
                 vx[row:row + TOK, 256 * p:256 * p + 128] = piece[:, C + 128 * p:C + 128 * p + 128]
 
-    def own_rows(slot):
-        return sb[slot, 0:TOK]
-
-    def far_rows(slot):
-        return sb[slot, TOK:2 * TOK]
+    def project_blocks(*blocks):
+        rows = [sb[s, 0:TOK] if far == 0 else sb[s, TOK:2 * TOK] for far, s in blocks]
+        project(rows[0] if len(rows) == 1 else jnp.concatenate(rows, axis=0), [ORDER.index(k) * TOK for k in blocks])
 
     loads[3].wait()
     loads[4].wait()
-    project(own_rows(0), [16 * TOK])
+    project_blocks((0, 0))
 
     tot = st_send[0]
     for j, cp in enumerate(stat1):
@@ -181,8 +185,7 @@
     for cp in stat2:
         cp.start()
     y_first.wait_recv()
-    half_p[1].start()
-    half_m[1].start()
+    send(2, 1)
 
     pe = iota((160, 256), 0)
     ps = iota((160, 256), 1)
@@ -197,13 +200,8 @@
     sel_left = jnp.where(left_ok & (ps == left_src), 1.0, 0.0).astype(BF16)
     sel_right = jnp.where(right_ok & (ps == right_src), 1.0, 0.0).astype(BF16)
 
-    own_p[1].wait_recv()
-    own_m[1].wait_recv()
-    own_p[2].start()
-    own_m[2].start()
-    ys[1].start()
-    ys[5].start()
-    project(jnp.concatenate([own_rows(1), own_rows(5)], axis=0), [TOK, 5 * TOK])
+    arrived(0, 1)
+    send(0, 2)
 
     tot = st_send[1]
     for j, cp in enumerate(stat2):
@@ -221,8 +219,12 @@
     gback = jnp.where((hc >= hl) & (hc < hl + per), 1.0, 0.0).astype(F32)
     wide = jnp.dot(both, gback, precision=HIGH, preferred_element_type=F32)
     xf = fresh[...].astype(F32)
-    v = (xf - wide[0:1]) * wide[1:2] * ngain[...]
+    v = (xf - wide[0:1]) * wide[1:2] * ngain[...].reshape(1, C)
     ext[16:16 + TOK, :] = (v * (1.0 / (1.0 + jnp.exp(-v)))).astype(BF16)
+    arrived(1, 1)
+    send(1, 2)
+    ys[1].start()
+    ys[5].start()
     for cp in halos:
         cp.wait_recv()
     zero = jnp.zeros((16, C), BF16)
@@ -241,7 +243,7 @@
     mean = jnp.mean(hidden, axis=-1, keepdims=True)
     cen = hidden - mean
     var = jnp.mean(cen * cen, axis=-1, keepdims=True)
-    normed = (cen * lax.rsqrt(var + 1e-05) * again[...]).astype(BF16)
+    normed = (cen * lax.rsqrt(var + 1e-05) * again[...].reshape(1, C)).astype(BF16)
     loads[6].wait()
     q_mine[...] = (jnp.dot(normed, wq[...], preferred_element_type=F32) * (LOG2E / 8)).astype(BF16)
     q_cp = {j: remote(q_mine, q_recv.at[NX - j - 1], q_ssem.at[j - 1], q_rsem.at[NX - j - 1], {"col": xn[j]})
@@ -250,80 +252,102 @@
         cp.start()
     project(normed, [0])
 
-    half_p[1].wait_recv()
-    half_m[1].wait_recv()
-    half_p[2].start()
-    half_m[2].start()
-    own_p[2].wait_recv()
-    own_m[2].wait_recv()
-    own_p[3].start()
-    own_m[3].start()
+    lane = iota((TOK, 128), 1)
+
+    def attend(slot, first, base, span, final):
+        q_ref = q_mine if slot == 0 else q_recv.at[slot - 1]
+        table = jnp.zeros((TOK, 128), F32)
+        for p in range(PAIRS):
+            qp = q_ref[:, 128 * p:128 * p + 128]
+            zq = jnp.zeros_like(qp)
+            qm = jnp.concatenate([jnp.where(lane < HEAD, qp, zq), jnp.where(lane < HEAD, zq, qp)], axis=0)
+            s = lax.dot_general(qm, kall[base:base + span, 128 * p:128 * p + 128], NT, preferred_element_type=F32)
+            m = jnp.max(s, axis=1, keepdims=True)
+            if not first:
+                before = st_m[slot, p][:, :1]
+                m = jnp.maximum(m, before)
+            w = jnp.exp2(s - m).astype(BF16)
+            o = jnp.dot(w, vx[base:base + span, 256 * p:256 * p + 256], preferred_element_type=F32)
+            if not first:
+                o = o + st_o[slot, p] * jnp.exp2(before - m)
+            if not final:
+                st_m[slot, p] = jnp.broadcast_to(m, (2 * TOK, 128))
+                st_o[slot, p] = o
+                continue
+            den = o[:, 128:]
+            norm = o[:, :128] / den
+            part[slot, :, 128 * p:128 * p + 128] = jnp.where(lane < HEAD, norm[:TOK], norm[TOK:]).astype(BF16)
+            ls = m + jnp.log2(den)
+            table = jnp.where(lane == 2 * p, ls[:TOK], jnp.where(lane == 2 * p + 1, ls[TOK:], table))
+        if final:
+            lse[slot] = table.T[:16]
+
+    def attend_a(slot):
+        attend(slot, True, 0 if slot == 0 else TOK, 8 * TOK, False)
+
+    def attend_b(slot):
+        attend(slot, False, 9 * TOK, 4 * TOK, False)
+
+    def attend_c(slot):
+        attend(slot, False, 13 * TOK, 4 * TOK, True)
+
+    arrived(2, 1)
+    send(2, 2)
+    arrived(0, 2)
+    send(0, 3)
+    project_blocks((0, 1), (0, 5))
+    arrived(1, 2)
+    send(1, 3)
     ys[2].start()
     ys[6].start()
-    project(jnp.concatenate([own_rows(2), own_rows(6)], axis=0), [2 * TOK, 6 * TOK])
-    half_p[2].wait_recv()
-    half_m[2].wait_recv()
-    half_p[3].start()
-    half_m[3].start()
-    own_p[3].wait_recv()
-    own_m[3].wait_recv()
-    own_p[4].start()
+    project_blocks((0, 2), (0, 6))
+    for s in (0, 1, 5):
+        ys[s].wait_recv()
+    project_blocks((1, 0), (1, 1), (1, 5))
+    attend_a(0)
+    arrived(0, 3)
+    send(0, 4)
+    arrived(2, 2)
+    send(2, 3)
+    arrived(1, 3)
+    send(1, 4)
     ys[3].start()
     ys[7].start()
-    project(jnp.concatenate([own_rows(3), own_rows(7)], axis=0), [3 * TOK, 7 * TOK])
-    half_m[3].wait_recv()
-    half_m[4].start()
-    half_p[3].wait_recv()
-    for s in (0, 1, 5):
+    project_blocks((0, 3), (0, 7))
+    for s in (2, 6):
         ys[s].wait_recv()
-    project(jnp.concatenate([far_rows(0), far_rows(1), far_rows(5)], axis=0), [8 * TOK, 9 * TOK, 13 * TOK])
-    own_p[4].wait_recv()
+    project_blocks((1, 2), (1, 6))
+    q_cp[NX - 1].wait_recv()
+    attend_a(1)
+    arrived(2, 3)
+    send(2, 4)
+    q_cp[NX - 3].wait_recv()
+    attend_a(3)
+    arrived(0, 4)
+    arrived(1, 4)
     ys[4].start()
-    for s in (2, 6, 3, 7):
+    attend_b(1)
+    attend_b(3)
+    q_cp[NX - 2].wait_recv()
+    attend_a(2)
+    attend_b(2)
+    for s in (3, 7):
         ys[s].wait_recv()
-    project(jnp.concatenate([far_rows(s) for s in (2, 6, 3, 7)], axis=0), [(8 + s) * TOK for s in (2, 6, 3, 7)])
-    half_m[4].wait_recv()
+    project_blocks((0, 4), (1, 3), (1, 7))
+    arrived(2, 4)
     ys[4].wait_recv()
-    project(jnp.concatenate([own_rows(4), far_rows(4)], axis=0), [4 * TOK, 12 * TOK])
-
-    lane = iota((TOK, 128), 1)
-
-    def attend(read_q, base, write, lse_ref):
-        table = jnp.zeros((TOK, 128), F32)
-        for p in range(PAIRS):
-            qp = read_q(p)
-            zq = jnp.zeros_like(qp)
-            qm = jnp.concatenate([jnp.where(lane < HEAD, qp, zq), jnp.where(lane < HEAD, zq, qp)], axis=0)
-            s = lax.dot_general(qm, kall[base:base + SPAN, 128 * p:128 * p + 128], NT, preferred_element_type=F32)
-            m = jnp.max(s, axis=1, keepdims=True)
-            w = jnp.exp2(s - m).astype(BF16)
-            o = jnp.dot(w, vx[base:base + SPAN, 256 * p:256 * p + 256], preferred_element_type=F32)
-            den = o[:, 128:]
-            norm = o[:, :128] / den
-            write(p, jnp.where(lane < HEAD, norm[:TOK], norm[TOK:]).astype(BF16))
-            ls = m + jnp.log2(den)
-            table = jnp.where(lane == 2 * p, ls[:TOK], jnp.where(lane == 2 * p + 1, ls[TOK:], table))
-        lse_ref[...] = table.T[:16]
-
-    def writer(ref):
-        def write(p, val):
-            ref[:, 128 * p:128 * p + 128] = val
-        return write
-
-    def reader(ref):
-        return lambda p: ref[:, 128 * p:128 * p + 128]
-
-    attend(reader(q_mine), 0, writer(part.at[0]), lse.at[0])
+    project_blocks((1, 4))
     backs = []
-    for j in (1, 3, 2):
-        q_cp[NX - j].wait_recv()
-        attend(reader(q_recv.at[j - 1]), TOK, writer(part.at[j]), lse.at[j])
+    for j in (2, 1, 3):
+        attend_c(j)
         dst = NX - j - 1
         a_cp = remote(part.at[j], ret_a.at[dst], a_ssem.at[j - 1], a_rsem.at[dst], {"col": xn[j]})
         l_cp = remote(lse.at[j], ret_l.at[dst], l_ssem.at[j - 1], l_rsem.at[dst], {"col": xn[j]})
         a_cp.start()
         l_cp.start()
         backs += [a_cp, l_cp]
+    attend_b(0)
+    attend_c(0)
     for cp in backs:
         cp.wait_recv()
 
@@ -347,8 +371,8 @@
     out = hid[...] + jnp.dot(att.astype(BF16), wo[...], preferred_element_type=F32)
     out_ref[...] = out.astype(BF16)
 
-    sends = stat1 + stat2 + halos + [y_first] + list(own_p.values()) + list(own_m.values())
-    sends += list(half_p.values()) + list(half_m.values()) + list(ys.values()) + list(q_cp.values()) + backs
+    sends = stat1 + stat2 + halos + [y_first] + [cp for some in ring.values() for cp in some]
+    sends += list(ys.values()) + list(q_cp.values()) + backs
     for cp in sends:
         cp.wait_send()
 
@@ -372,15 +396,16 @@
             V((NZ, 2 * TOK, C), BF16), V((KROWS, C), BF16), V((KROWS, 256 * PAIRS), BF16), V((TOK, C), F32),
             V((TOK, C), BF16), V((3, TOK, C), BF16), V((4, TOK, C), BF16), V((3, TOK, C), BF16),
             V((4, 16, 128), F32), V((3, 16, 128), F32),
+            V((4, PAIRS, 2 * TOK, 256), F32), V((4, PAIRS, 2 * TOK, 128), F32),
             dma((8,)), dma((2, 7)), dma((2, 7)), dma((8,)), dma((8,)),
-            dma((8,)), dma((8,)), dma((8,)), dma((8,)), dma((9,)), dma((9,)),
+            dma((3, 2, 4)), dma((3, 2, 4)), dma((9,)), dma((9,)),
             dma((3,)), dma((3,)), dma((3,)), dma((3,)), dma((3,)), dma((3,)),
         ],
         compiler_params=pltpu.CompilerParams(
             collective_id=0, has_side_effects=True, vmem_limit_bytes=60 * 2**20),
     )(
         flat(fresh), flat(stale_conv_in), flat(stale_normed),
-        norm_gain.reshape(1, C), attn_gain.reshape(1, C),
+        norm_gain, attn_gain,
         conv_weight.reshape(9 * C, C), w_query, w_key, w_value, w_out,
     )
     return out.reshape(shape)

time: 64.4 us -> 55.2 us (0.86)
  Pallas kernels: 60.1 us -> 53.4 us
  local copies, waits for them, and re-layouts: 4.11 us -> 1.6 us
    pallas_call x1, Pallas kernels: 60.1 us -> 53.4 us  [on_device(): pl.pallas_call(kernel, out_shape=jax.ShapeDtypeStruct((TOK, C), BF16), in...]
    reshape x2 -> x0, local copies, waits for them, and re-layouts: 2.51 us -> none  [the longest x1 1.27 us: on_device(): norm_gain.reshape(1, C)]
where the time goes in v2:
time: 55.2 us; the launch traced here: 55.1 us
  Pallas kernels  53.4 us (97%)
  local copies, waits for them, and re-layouts  1.6 us (3%)
    pallas_call x1, Pallas kernels, on_device(): pl.pallas_call(kernel, out_shape=jax.ShapeDtypeStruct((TOK, C), BF16), in...  53.4 us
    unnamed x1, local copies, waits for them, and re-layouts  1.6 us

profile of v2, /device:TPU:16, one launch (start us, length us, event | category | flops | bytes accessed | tf_op | source)
XLA Modules:
  0.0 55.1 jit_solution(14619364473286074986)
XLA Ops:
  0.0 53.4 %shard_map.100 = bf16[128,640]{1,0:T(8,128)(2,1)} custom-call(bf16[128,640]{1,0:T(8,128)(2,1)} %bitcast.7, bf16[128,640]{1,0:T(8,128)(2,1)} %bitcast.8, bf16[128,640]{1,0:T(8,128)(2,1)} %bitcast.9, f32[640]{0:T(1024)} %ngain.1, f32[640]{0:T(1024)} %again.1, bf16[5760,640]{1,0:T(8,128)(2,1)} %bitcast.5, bf16[640,640]{1,0:T(8,128)(2,1)} %wq_h.1, ...), custom_call_target="tpu_custom_call" | custom-call | tf_op jit(solution)/shard_map/pallas_call | solution.py:387
  53.5 1.6 %copy.12 = bf16[8,16,640]{2,1,0:T(8,128)(2,1)} copy(bf16[8,16,640]{2,1,0:T(8,128)(2,1)} %bitcast.6) | data formatting | bytes 327680

commit v3 on v2

--- a/solution.py
+++ b/solution.py
@@ -139,7 +139,7 @@
         for cp in ring[stream, step]:
             cp.wait_recv()
 
-    send(0, 1)
+    send(1, 1)
     y_first.start()
 
     lft, rgt = coln[NCOL - 1], coln[1]
@@ -154,7 +154,7 @@
              for i, (src, at, dev) in enumerate(plan)]
     for cp in halos:
         cp.start()
-    send(1, 1)
+    send(0, 1)
     ys[0].start()
 
     for p in range(PAIRS):
@@ -200,6 +200,10 @@
     sel_left = jnp.where(left_ok & (ps == left_src), 1.0, 0.0).astype(BF16)
     sel_right = jnp.where(right_ok & (ps == right_src), 1.0, 0.0).astype(BF16)
 
+    arrived(1, 1)
+    send(1, 2)
+    ys[1].start()
+    ys[5].start()
     arrived(0, 1)
     send(0, 2)
 
@@ -221,10 +225,6 @@
     xf = fresh[...].astype(F32)
     v = (xf - wide[0:1]) * wide[1:2] * ngain[...].reshape(1, C)
     ext[16:16 + TOK, :] = (v * (1.0 / (1.0 + jnp.exp(-v)))).astype(BF16)
-    arrived(1, 1)
-    send(1, 2)
-    ys[1].start()
-    ys[5].start()
     for cp in halos:
         cp.wait_recv()
     zero = jnp.zeros((16, C), BF16)
@@ -248,16 +248,26 @@
     q_mine[...] = (jnp.dot(normed, wq[...], preferred_element_type=F32) * (LOG2E / 8)).astype(BF16)
     q_cp = {j: remote(q_mine, q_recv.at[NX - j - 1], q_ssem.at[j - 1], q_rsem.at[NX - j - 1], {"col": xn[j]})
             for j in (1, 3, 2)}
-    for cp in q_cp.values():
-        cp.start()
+    q_cp[1].start()
+    q_cp[3].start()
+    arrived(1, 2)
+    send(1, 3)
+    ys[2].start()
+    ys[6].start()
+    arrived(0, 2)
+    send(0, 3)
+    arrived(2, 1)
+    send(2, 2)
+    q_cp[2].start()
     project(normed, [0])
 
     lane = iota((TOK, 128), 1)
 
-    def attend(slot, first, base, span, final):
+    def attend(slot, base, span, pairs=range(PAIRS), first=True, final=False, table=None):
         q_ref = q_mine if slot == 0 else q_recv.at[slot - 1]
-        table = jnp.zeros((TOK, 128), F32)
-        for p in range(PAIRS):
+        if table is None:
+            table = jnp.zeros((TOK, 128), F32)
+        for p in pairs:
             qp = q_ref[:, 128 * p:128 * p + 128]
             zq = jnp.zeros_like(qp)
             qm = jnp.concatenate([jnp.where(lane < HEAD, qp, zq), jnp.where(lane < HEAD, zq, qp)], axis=0)
@@ -281,73 +291,65 @@
             table = jnp.where(lane == 2 * p, ls[:TOK], jnp.where(lane == 2 * p + 1, ls[TOK:], table))
         if final:
             lse[slot] = table.T[:16]
-
-    def attend_a(slot):
-        attend(slot, True, 0 if slot == 0 else TOK, 8 * TOK, False)
-
-    def attend_b(slot):
-        attend(slot, False, 9 * TOK, 4 * TOK, False)
-
-    def attend_c(slot):
-        attend(slot, False, 13 * TOK, 4 * TOK, True)
-
-    arrived(2, 1)
-    send(2, 2)
-    arrived(0, 2)
-    send(0, 3)
-    project_blocks((0, 1), (0, 5))
-    arrived(1, 2)
-    send(1, 3)
-    ys[2].start()
-    ys[6].start()
-    project_blocks((0, 2), (0, 6))
+        return table
+
+    project_blocks((0, 1), (0, 5), (0, 2), (0, 6))
     for s in (0, 1, 5):
         ys[s].wait_recv()
     project_blocks((1, 0), (1, 1), (1, 5))
-    attend_a(0)
+    attend(0, 0, 8 * TOK)
+    arrived(1, 3)
+    send(1, 4)
+    ys[3].start()
+    ys[7].start()
     arrived(0, 3)
     send(0, 4)
     arrived(2, 2)
     send(2, 3)
-    arrived(1, 3)
-    send(1, 4)
-    ys[3].start()
-    ys[7].start()
-    project_blocks((0, 3), (0, 7))
-    for s in (2, 6):
-        ys[s].wait_recv()
-    project_blocks((1, 2), (1, 6))
+    ys[2].wait_recv()
+    ys[6].wait_recv()
+    project_blocks((0, 3), (0, 7), (1, 2), (1, 6))
     q_cp[NX - 1].wait_recv()
-    attend_a(1)
+    attend(1, TOK, 12 * TOK)
+    arrived(1, 4)
+    ys[4].start()
+    arrived(0, 4)
     arrived(2, 3)
     send(2, 4)
+    ys[3].wait_recv()
+    ys[7].wait_recv()
+    project_blocks((0, 4), (1, 3), (1, 7))
     q_cp[NX - 3].wait_recv()
-    attend_a(3)
-    arrived(0, 4)
-    arrived(1, 4)
-    ys[4].start()
-    attend_b(1)
-    attend_b(3)
-    q_cp[NX - 2].wait_recv()
-    attend_a(2)
-    attend_b(2)
-    for s in (3, 7):
-        ys[s].wait_recv()
-    project_blocks((0, 4), (1, 3), (1, 7))
+    attend(3, TOK, 12 * TOK)
     arrived(2, 4)
     ys[4].wait_recv()
     project_blocks((1, 4))
     backs = []
-    for j in (2, 1, 3):
-        attend_c(j)
+
+    def give_back(j, g, at, wide_g):
         dst = NX - j - 1
-        a_cp = remote(part.at[j], ret_a.at[dst], a_ssem.at[j - 1], a_rsem.at[dst], {"col": xn[j]})
-        l_cp = remote(lse.at[j], ret_l.at[dst], l_ssem.at[j - 1], l_rsem.at[dst], {"col": xn[j]})
-        a_cp.start()
-        l_cp.start()
-        backs += [a_cp, l_cp]
-    attend_b(0)
-    attend_c(0)
+        cp = remote(part.at[j, :, pl.ds(at, wide_g)], ret_a.at[dst, :, pl.ds(at, wide_g)],
+                    a_ssem.at[j - 1, g], a_rsem.at[dst, g], {"col": xn[j]})
+        cp.start()
+        backs.append(cp)
+
+    def give_lse(j):
+        dst = NX - j - 1
+        cp = remote(lse.at[j], ret_l.at[dst], l_ssem.at[j - 1], l_rsem.at[dst], {"col": xn[j]})
+        cp.start()
+        backs.append(cp)
+
+    for j in (1, 3):
+        attend(j, 13 * TOK, 4 * TOK, first=False, final=True)
+        give_back(j, 0, 0, C)
+        give_lse(j)
+    q_cp[NX - 2].wait_recv()
+    table = attend(2, TOK, 16 * TOK, range(0, 3), final=True)
+    give_back(2, 0, 0, 384)
+    attend(2, TOK, 16 * TOK, range(3, PAIRS), final=True, table=table)
+    give_back(2, 1, 384, 256)
+    give_lse(2)
+    attend(0, 9 * TOK, 8 * TOK, first=False, final=True)
     for cp in backs:
         cp.wait_recv()
 
@@ -399,7 +401,7 @@
             V((4, PAIRS, 2 * TOK, 256), F32), V((4, PAIRS, 2 * TOK, 128), F32),
             dma((8,)), dma((2, 7)), dma((2, 7)), dma((8,)), dma((8,)),
             dma((3, 2, 4)), dma((3, 2, 4)), dma((9,)), dma((9,)),
-            dma((3,)), dma((3,)), dma((3,)), dma((3,)), dma((3,)), dma((3,)),
+            dma((3,)), dma((3,)), dma((3, 2)), dma((3, 2)), dma((3,)), dma((3,)),
         ],
         compiler_params=pltpu.CompilerParams(
             collective_id=0, has_side_effects=True, vmem_limit_bytes=60 * 2**20),

time: 55.2 us -> 52.6 us (0.953)
  Pallas kernels: 53.4 us -> 50.9 us
    pallas_call x1, Pallas kernels: 53.4 us -> 50.9 us  [on_device(): pl.pallas_call(kernel, out_shape=jax.ShapeDtypeStruct((TOK, C), BF16), in...]
where the time goes in v3:
time: 52.6 us; the launch traced here: 52.5 us
  Pallas kernels  50.9 us (97%)
  local copies, waits for them, and re-layouts  1.6 us (3%)
    pallas_call x1, Pallas kernels, on_device(): pl.pallas_call(kernel, out_shape=jax.ShapeDtypeStruct((TOK, C), BF16), in...  50.9 us
    unnamed x1, local copies, waits for them, and re-layouts  1.6 us

profile of v3, /device:TPU:16, one launch (start us, length us, event | category | flops | bytes accessed | tf_op | source)
XLA Modules:
  0.0 52.5 jit_solution(16425408582488874856)
XLA Ops:
  0.0 50.9 %shard_map.100 = bf16[128,640]{1,0:T(8,128)(2,1)} custom-call(bf16[128,640]{1,0:T(8,128)(2,1)} %bitcast.7, bf16[128,640]{1,0:T(8,128)(2,1)} %bitcast.8, bf16[128,640]{1,0:T(8,128)(2,1)} %bitcast.9, f32[640]{0:T(1024)} %ngain.1, f32[640]{0:T(1024)} %again.1, bf16[5760,640]{1,0:T(8,128)(2,1)} %bitcast.5, bf16[640,640]{1,0:T(8,128)(2,1)} %wq_h.1, ...), custom_call_target="tpu_custom_call" | custom-call | tf_op jit(solution)/shard_map/pallas_call | solution.py:389
  50.9 1.6 %copy.12 = bf16[8,16,640]{2,1,0:T(8,128)(2,1)} copy(bf16[8,16,640]{2,1,0:T(8,128)(2,1)} %bitcast.6) | data formatting | bytes 327680

commit v4 on v3

--- a/solution.py
+++ b/solution.py
@@ -248,8 +248,8 @@
     q_mine[...] = (jnp.dot(normed, wq[...], preferred_element_type=F32) * (LOG2E / 8)).astype(BF16)
     q_cp = {j: remote(q_mine, q_recv.at[NX - j - 1], q_ssem.at[j - 1], q_rsem.at[NX - j - 1], {"col": xn[j]})
             for j in (1, 3, 2)}
-    q_cp[1].start()
     q_cp[3].start()
+    q_cp[2].start()
     arrived(1, 2)
     send(1, 3)
     ys[2].start()
@@ -258,7 +258,7 @@
     send(0, 3)
     arrived(2, 1)
     send(2, 2)
-    q_cp[2].start()
+    q_cp[1].start()
     project(normed, [0])
 
     lane = iota((TOK, 128), 1)
@@ -319,8 +319,8 @@
     ys[3].wait_recv()
     ys[7].wait_recv()
     project_blocks((0, 4), (1, 3), (1, 7))
-    q_cp[NX - 3].wait_recv()
-    attend(3, TOK, 12 * TOK)
+    q_cp[NX - 2].wait_recv()
+    attend(2, TOK, 12 * TOK)
     arrived(2, 4)
     ys[4].wait_recv()
     project_blocks((1, 4))
@@ -339,16 +339,16 @@
         cp.start()
         backs.append(cp)
 
-    for j in (1, 3):
+    for j in (2, 1):
         attend(j, 13 * TOK, 4 * TOK, first=False, final=True)
         give_back(j, 0, 0, C)
         give_lse(j)
-    q_cp[NX - 2].wait_recv()
-    table = attend(2, TOK, 16 * TOK, range(0, 3), final=True)
-    give_back(2, 0, 0, 384)
-    attend(2, TOK, 16 * TOK, range(3, PAIRS), final=True, table=table)
-    give_back(2, 1, 384, 256)
-    give_lse(2)
+    q_cp[NX - 3].wait_recv()
+    table = attend(3, TOK, 16 * TOK, range(0, 3), final=True)
+    give_back(3, 0, 0, 384)
+    attend(3, TOK, 16 * TOK, range(3, PAIRS), final=True, table=table)
+    give_back(3, 1, 384, 256)
+    give_lse(3)
     attend(0, 9 * TOK, 8 * TOK, first=False, final=True)
     for cp in backs:
         cp.wait_recv()

time: 52.6 us -> 51.6 us (0.981)
  Pallas kernels: 50.9 us -> 49.5 us
    pallas_call x1, Pallas kernels: 50.9 us -> 49.5 us  [on_device(): pl.pallas_call(kernel, out_shape=jax.ShapeDtypeStruct((TOK, C), BF16), in...]
where the time goes in v4:
time: 51.6 us; the launch traced here: 51.1 us
  Pallas kernels  49.5 us (96%)
  local copies, waits for them, and re-layouts  1.6 us (3%)
    pallas_call x1, Pallas kernels, on_device(): pl.pallas_call(kernel, out_shape=jax.ShapeDtypeStruct((TOK, C), BF16), in...  49.5 us
    unnamed x1, local copies, waits for them, and re-layouts  1.6 us

profile of v4, /device:TPU:16, one launch (start us, length us, event | category | flops | bytes accessed | tf_op | source)
XLA Modules:
  0.0 51.1 jit_solution(18431568217859654947)
XLA Ops:
  0.0 49.5 %shard_map.100 = bf16[128,640]{1,0:T(8,128)(2,1)} custom-call(bf16[128,640]{1,0:T(8,128)(2,1)} %bitcast.7, bf16[128,640]{1,0:T(8,128)(2,1)} %bitcast.8, bf16[128,640]{1,0:T(8,128)(2,1)} %bitcast.9, f32[640]{0:T(1024)} %ngain.1, f32[640]{0:T(1024)} %again.1, bf16[5760,640]{1,0:T(8,128)(2,1)} %bitcast.5, bf16[640,640]{1,0:T(8,128)(2,1)} %wq_h.1, ...), custom_call_target="tpu_custom_call" | custom-call | tf_op jit(solution)/shard_map/pallas_call | solution.py:389
  49.5 1.6 %copy.12 = bf16[8,16,640]{2,1,0:T(8,128)(2,1)} copy(bf16[8,16,640]{2,1,0:T(8,128)(2,1)} %bitcast.6) | data formatting | bytes 327680
